TPU v7x, 32 devices: a whole 2x2x4 slice. The times are simulated.
32 devices in a mesh: tile: 8 (over z, x), lev: 4 (over y, core).
Axes of the slice: x: 2, y: 2, z: 4, core: 2. Of those that a mesh axis runs over, the one named last changes fastest.
Arguments:
- theta: float32 [128, 32, 1024], P('lev', None, 'tile'), may hold values from -6 to 6
- thickness: float32 [128, 32, 1024], P('lev', None, 'tile'), may hold values from 0.5 to 1.5
- wind: float32 [128, 32, 1024], P('lev', None, 'tile'), may hold values from -6 to 6
- surface: float32 [32, 1024], P(None, 'tile'), may hold values from -6 to 6
- trigger: int32 [32, 1024], P(None, 'tile'), may hold values 0 or 1
- closure: int32 [32, 1024], P(None, 'tile'), may hold values from 0 to 2
- closure_weights: bfloat16 [4, 128, 128], replicated, may hold values from -0.5 to 0.5
Outputs:
- pressure: float32 [128, 32, 1024], P('lev', None, 'tile')
- wind_next: float32 [128, 32, 1024], P('lev', None, 'tile')
- heating: bfloat16 [128, 32, 1024], P('lev', None, 'tile')
Inputs may be any that keep to these rules, and one draw needn't show every extreme that they name: trigger[r, c] is 0 or 1 in every draw. closure[r, c] is one of 0 .. 2 in every draw.
All inputs are finite; a program needn't handle non-finite values. No bound on the sum of `trigger` on one device may be relied on, other than what follows from the above.
Results may differ from a plain program's by a relative error of at most 0.0049.
Values may be sent and summed in bfloat16 or wider, within the bound.
A program may use at most 64 MiB of HBM per device.

v0:
```python
import jax
import jax.numpy as jnp
from jax import lax
from jax.sharding import PartitionSpec as P

LEVELS = 128
SUBSTEPS = 6


courant = 0.9


def carried_in(value, axis, join, neutral):
    count, mine = (lax.axis_size(axis), lax.axis_index(axis))
    pieces = lax.all_gather(value, axis)
    pieces = pieces[::-1]
    mine = count - 1 - mine
    subtotal = jnp.full_like(value, 0) + jnp.asarray(neutral, value.dtype)

    def step(position, subtotal):
        longer = join(subtotal, pieces[position])
        return jnp.where(position < mine, longer, subtotal)

    return lax.fori_loop(0, count - 1, step, subtotal)


def with_halo(cells, sides, width):
    for axis, dim in sides:
        count = lax.axis_size(axis)
        head = lax.slice_in_dim(cells, 0, width, axis=dim)
        tail = lax.slice_in_dim(cells, cells.shape[dim] - width, cells.shape[dim], axis=dim)
        cells = jnp.concatenate(
            [
                lax.ppermute(tail, axis, [(i, (i + 1) % count) for i in range(count)]),
                cells,
                lax.ppermute(head, axis, [((i + 1) % count, i) for i in range(count)]),
            ],
            axis=dim,
        )
    return cells


def add_pair(earlier, later):
    return earlier + later


def advance(extended):
    pressure = extended[0]
    velocity = extended[1]
    velocity = velocity[:, :, :-1] - courant * (pressure[:, :, 1:] - pressure[:, :, :-1])
    pressure = pressure[:, :, 1:-1] - courant * (velocity[:, :, 1:] - velocity[:, :, :-1])
    return jnp.stack([pressure, velocity[:, :, 1:]])


def combine_heating(products, triggers_here, closures_here):
    schemes = products.shape[0] - 1
    onehot = (
        closures_here[None, :, :] == jnp.arange(schemes, dtype=jnp.int32)[:, None, None]
    ).astype(jnp.float32)
    convect = jnp.sum(products[:schemes] * onehot[:, None, :, :], axis=0)
    return products[schemes] + triggers_here.astype(jnp.float32)[None, :, :] * convect


def shards(theta, thickness, wind, surface, trigger, closure, closure_weights):
    row_count = theta.shape[1]
    longitudes = theta.shape[2]
    lev_count = lax.axis_size("lev")
    lev_rank = lax.axis_index("lev")
    thermal = theta * thickness * LEVELS ** (-0.5)
    column_total = jnp.sum(thermal, axis=0)
    higher = carried_in(column_total, "lev", add_pair, jnp.zeros_like(column_total))
    suffix = lax.cumsum(thermal, axis=0, reverse=True) - thermal
    geopot = surface[None, :, :] + higher[None, :, :] + suffix + 0.5 * thermal
    fields = jnp.stack([geopot, wind])
    extended = with_halo(fields, (("tile", 3),), SUBSTEPS)
    for substep in range(SUBSTEPS):
        extended = advance(extended)
    fields = extended
    local_theta = theta.astype(jnp.bfloat16)
    portion = longitudes // lev_count
    whole_columns = lax.all_to_all(local_theta, "lev", split_axis=2, concat_axis=0, tiled=True)
    triggers_here = lax.dynamic_slice_in_dim(trigger, lev_rank * portion, portion, 1)
    closures_here = lax.dynamic_slice_in_dim(closure, lev_rank * portion, portion, 1)
    stacked = closure_weights.reshape(
        (closure_weights.shape[0] * closure_weights.shape[1], closure_weights.shape[2])
    )
    flat_columns = whole_columns.reshape((whole_columns.shape[0], row_count * portion))
    products = jnp.dot(stacked, flat_columns, preferred_element_type=jnp.float32)
    products = products.reshape(
        (closure_weights.shape[0], closure_weights.shape[1], row_count, portion)
    )
    heat_cols = combine_heating(products, triggers_here, closures_here).astype(jnp.bfloat16)
    heating = lax.all_to_all(heat_cols, "lev", split_axis=0, concat_axis=2, tiled=True)
    return (fields[0], fields[1], heating)


def solution(mesh):
    in_specs = (
        P("lev", None, "tile"),
        P("lev", None, "tile"),
        P("lev", None, "tile"),
        P(None, "tile"),
        P(None, "tile"),
        P(None, "tile"),
        P(),
    )
    out_specs = (P("lev", None, "tile"), P("lev", None, "tile"), P("lev", None, "tile"))
    return jax.shard_map(shards, mesh=mesh, in_specs=in_specs, out_specs=out_specs, check_vma=False)
```

profile of v0, /device:TPU:0, one launch (start us, length us, event | category | flops | bytes accessed | tf_op | source)
XLA Modules:
  0.0 63.5 jit_solution(4351620419405802746)
XLA Ops:
  0.6 0.0 copy-start
  0.6 0.0 copy-start.1
  0.7 0.0 copy-start.2
  0.7 0.0 copy-start.4
  0.7 1.6 %fusion.32 = (bf16[32,32,128]{2,1,0:T(8,128)(2,1)S(1)}, f32[32,128]{1,0:T(8,128)S(1)}) fusion(f32[32,32,128]{2,1,0:T(8,128)} %param.9, f32[32,32,128]{2,1,0:T(8,128)} %param.10), kind=kLoop, calls=%fused_computation.57 | loop fusion | flops 520192 | bytes 1327104 | tf_op jit(solution)/shard_map/convert_element_type | solution.py:79
  2.3 6.2 %all-gather = f32[128,128]{1,0:T(8,128)S(1)} all-gather(f32[32,128]{1,0:T(8,128)S(1)} %get-tuple-element.113), channel_id=2, replica_groups=mesh['tile'=8,'lev'=4] {'lev'}, dimensions={0}, use_global_device_ids=true | all-gather | bytes 81920 | tf_op jit(solution)/shard_map/all_gather | solution.py:15
  8.5 0.1 while.14
  8.6 0.7 %add.50 = f32[32,128]{1,0:T(8,128)S(1)} add(f32[32,128]{1,0:T(8,128)} %param.12, f32[32,128]{1,0:T(8,128)S(1)} %get-tuple-element.82) | non-fusion elementwise | flops 4096 | bytes 49152 | tf_op jit(solution)/shard_map/add | solution.py:73
  9.4 0.0 copy-done.1
  9.4 0.0 copy-done.2
  9.4 0.5 fusion.24
  9.9 0.0 copy-done.4
  9.9 0.4 slice_maximum_fusion
  10.3 1.2 %copy.26 = f32[2,32,32,6]{2,1,3,0:T(8,128)} copy(f32[2,32,32,6]{3,2,1,0:T(8,128)S(1)} %get-tuple-element.111) | data formatting | bytes 98304 | tf_op jit(solution)/shard_map/slice | solution.py:30
  11.5 5.0 %collective-permute-start.1 = (f32[2,32,32,6]{2,1,3,0:T(8,128)}, f32[2,32,32,6]{2,1,3,0:T(8,128)S(1)}, u32[]{:S(2)}, u32[]{:S(2)}) collective-permute-start(f32[2,32,32,6]{2,1,3,0:T(8,128)} %copy.26), channel_id=1, source_target_pairs={{4,0},{8,4},{12,8},{16,12},{20,16},{24,20},{28,24},{0,28},{5,1},{9... | collective-permute-start | bytes 147464 | tf_op jit(solution)/shard_map/ppermute | solution.py:36
  16.5 0.6 copy.25
  17.1 0.1 collective-permute-start
  17.2 1.4 %copy.29 = bf16[32,32,128]{1,0,2:T(8,128)(2,1)S(1)} copy(bf16[32,32,128]{2,1,0:T(8,128)(2,1)S(1)} %get-tuple-element.112) | data formatting | bytes 524288 | tf_op jit(solution)/shard_map/convert_element_type | solution.py:79
  18.6 1.7 %reshape.28 = bf16[4,2,16384]{2,1,0:T(2,128)(2,1)} reshape(bf16[128,32,32]{2,1,0:T(8,128)(2,1)S(1)} %bitcast.28) | data formatting | bytes 524288
  20.3 3.6 %all-to-all-start = ((bf16[4,2,16384]{2,1,0:T(2,128)(2,1)}), bf16[4,2,16384]{2,1,0:T(2,128)(2,1)S(1)}, u32[]{:S(2)}, u32[]{:S(2)}) async-start(bf16[4,2,16384]{2,1,0:T(2,128)(2,1)} %reshape.28), calls=%async_computation | async-start | bytes 524288 | tf_op jit(solution)/shard_map/all_to_all | solution.py:81
  23.9 0.0 copy-done.6
  23.9 0.0 copy-done.7
  23.9 0.1 dynamic-slice_convert_fusion
  24.0 1.0 %fusion.27 = f32[3,32,32]{0,2,1:T(8,128)} fusion(s32[32,32]{1,0:T(8,128)S(1)} %get-tuple-element.115), kind=kLoop, calls=%fused_computation.49 | loop fusion | flops 6144 | bytes 16384 | tf_op jit(solution)/shard_map/convert_element_type | solution.py:59
  25.0 0.0 collective-permute-done.1
  25.0 0.5 copy.28
  25.5 1.4 %collective-permute-done = f32[2,32,32,6]{2,1,3,0:T(8,128)} collective-permute-done((f32[2,32,32,6]{2,1,3,0:T(8,128)S(1)}, f32[2,32,32,6]{2,1,3,0:T(8,128)}, u32[]{:S(2)}, u32[]{:S(2)}) %collective-permute-start) | collective-permute-done | bytes 49184 | tf_op jit(solution)/shard_map/ppermute | solution.py:34
  26.8 1.4 %copy.27 = f32[2,32,32,6]{3,2,1,0:T(8,128)S(1)} copy(f32[2,32,32,6]{2,1,3,0:T(8,128)} %collective-permute-done) | data formatting | bytes 98304 | tf_op jit(solution)/shard_map/ppermute | solution.py:34
  28.2 0.9 %pad_maximum_fusion = f32[2,32,32,140]{3,2,1,0:T(8,128)S(1)} fusion(f32[2,32,32,6]{3,2,1,0:T(8,128)S(1)} %copy.28, f32[1,32,32,128]{3,2,1,0:T(8,128)S(1)} %bitcast.33, f32[1,32,32,128]{3,2,1,0:T(8,128)S(1)} %fusion.24, f32[2,32,32,6]{3,2,1,0:T(8,128)S(1)} %copy.27), kind=kLoop, calls=%fused_computation.1 | loop fusion | flops 860160 | bytes 2293760 | tf_op jit(solution)/shard_map/concatenate | solution.py:32
  29.1 0.2 slice_bitcast_fusion
  29.3 0.4 fusion.21
  29.7 0.6 fusion.19
  30.3 0.6 fusion.17
  30.9 0.6 fusion.15
  31.6 0.6 fusion.13
  32.2 0.6 fusion.11
  32.8 0.6 fusion.9
  33.4 0.6 fusion.7
  34.0 0.6 fusion.5
  34.6 0.6 fusion.3
  35.2 1.6 %fusion.1 = f32[32,32,129]{2,1,0:T(8,128)} fusion(f32[32,32,130]{2,1,0:T(8,128)S(1)} %fusion.3, f32[32,32,131]{2,1,0:T(8,128)S(1)} %fusion.5), kind=kLoop, calls=%fused_computation.5 | loop fusion | flops 396288 | bytes 2113536 | tf_op jit(solution)/shard_map/sub | solution.py:50
  36.9 0.0 all-to-all-done
  36.9 0.5 reshape.29
  37.4 1.2 %copy.30 = bf16[32,32,4,32]{3,1,0,2:T(8,128)(2,1)S(1)} copy(bf16[32,32,4,32]{1,0,3,2:T(8,128)(2,1)S(1)} %bitcast.29) | data formatting | bytes 524288 | tf_op jit(solution)/shard_map/all_to_all | solution.py:81
  38.6 1.1 %reshape.26 = bf16[128,1024]{1,0:T(8,128)(2,1)S(1)} reshape(bf16[4,32,32,32]{3,2,1,0:T(8,128)(2,1)S(1)} %bitcast.30) | data formatting | bytes 524288 | tf_op jit(solution)/shard_map/reshape | solution.py:87
  39.7 0.0 copy-done
  39.7 0.4 fusion.33
  40.2 0.2 slice.225
  40.3 1.0 %copy.31 = f32[128,1024]{0,1:T(8,128)} copy(f32[128,1024]{1,0:T(8,128)S(1)} %slice.224) | data formatting | bytes 1048576 | tf_op jit(solution)/shard_map/slice | solution.py:61
  41.3 1.6 %copy.32 = f32[384,1024]{0,1:T(8,128)} copy(f32[384,1024]{1,0:T(8,128)S(1)} %slice.225) | data formatting | bytes 3145728 | tf_op jit(solution)/shard_map/slice | solution.py:60
  43.0 2.5 %slice.183 = f32[3,128,32,32]{1,0,3,2:T(4,128)S(1)} reshape(f32[384,1024]{0,1:T(8,128)} %copy.32) | data formatting | bytes 3145728 | tf_op jit(solution)/shard_map/slice | solution.py:60
  45.5 0.0 copy-start.5
  45.5 2.7 %multiply_reduce_fusion = f32[128,32,32]{0,2,1:T(8,128)S(1)} fusion(f32[3,128,32,32]{1,0,3,2:T(4,128)S(1)} %slice.183, f32[3,32,32]{0,2,1:T(8,128)} %fusion.27), kind=kLoop, calls=%fused_computation.2 | loop fusion | flops 655360 | bytes 2109440 | tf_op jit(solution)/shard_map/reduce_sum | solution.py:60
  48.2 0.0 copy-done.5
  48.2 0.0 copy-start.3
  48.2 0.2 add_convert_fusion
  48.4 1.4 %copy.33 = bf16[128,32,32]{2,1,0:T(8,128)(2,1)S(1)} copy(bf16[128,32,32]{0,2,1:T(8,128)(2,1)S(1)} %add_convert_fusion) | data formatting | bytes 524288 | tf_op jit(solution)/shard_map/convert_element_type | solution.py:92
  49.9 1.7 %reshape.30 = bf16[4,2,16384]{2,1,0:T(2,128)(2,1)} reshape(bf16[128,32,32]{2,1,0:T(8,128)(2,1)S(1)} %copy.33) | data formatting | bytes 524288
  51.6 3.4 %all-to-all-start.1 = ((bf16[4,2,16384]{2,1,0:T(2,128)(2,1)}), bf16[4,2,16384]{2,1,0:T(2,128)(2,1)S(1)}, u32[]{:S(2)}, u32[]{:S(2)}) async-start(bf16[4,2,16384]{2,1,0:T(2,128)(2,1)} %reshape.30), calls=%async_computation.1 | async-start | bytes 524288 | tf_op jit(solution)/shard_map/all_to_all | solution.py:93
  55.0 1.3 %fusion.26 = (f32[32,32,128]{2,1,0:T(8,128)}, f32[32,32,128]{2,1,0:T(8,128)}) fusion(f32[32,32,129]{2,1,0:T(8,128)S(1)} %copy-done.3, f32[32,32,130]{2,1,0:T(8,128)S(1)} %fusion.3), kind=kLoop, calls=%fused_computation.46 | loop fusion | flops 393216 | bytes 2621440 | tf_op jit(solution)/shard_map/sub | solution.py:51
  56.3 4.7 %all-to-all-done.1 = bf16[4,2,16384]{2,1,0:T(2,128)(2,1)S(1)} async-done(((bf16[4,2,16384]{2,1,0:T(2,128)(2,1)}), bf16[4,2,16384]{2,1,0:T(2,128)(2,1)S(1)}, u32[]{:S(2)}, u32[]{:S(2)}) %all-to-all-start.1) | async-done | bytes 262176 | tf_op jit(solution)/shard_map/all_to_all | solution.py:93
  61.0 0.5 reshape.31
  61.5 0.8 %copy.34 = bf16[32,32,4,32]{3,2,1,0:T(4,128)(2,1)S(1)} copy(bf16[32,32,4,32]{3,1,0,2:T(8,128)(2,1)S(1)} %bitcast.31) | data formatting | bytes 524288 | tf_op jit(solution)/shard_map/all_to_all | solution.py:93
  62.3 1.2 %all_to_all.30 = bf16[32,32,128]{2,1,0:T(8,128)(2,1)} reshape(bf16[32,32,4,32]{3,2,1,0:T(4,128)(2,1)S(1)} %copy.34) | data formatting | bytes 524288 | tf_op jit(solution)/shard_map/all_to_all | solution.py:93
  (9 shorter events, 0.1 us)
Async XLA Ops:
  0.6 39.0 %copy-start = (bf16[4,128,128]{2,1,0:T(8,128)(2,1)S(1)}, bf16[4,128,128]{2,1,0:T(8,128)(2,1)}, u32[]{:S(2)}) copy-start(bf16[4,128,128]{2,1,0:T(8,128)(2,1)} %param.15) | copy-start | bytes 393220
  0.6 8.7 %copy-start.1 = (f32[32,32,128]{2,1,0:T(8,128)S(1)}, f32[32,32,128]{2,1,0:T(8,128)}, u32[]{:S(2)}) copy-start(f32[32,32,128]{2,1,0:T(8,128)} %param.9) | copy-start | bytes 1572868
  0.7 8.7 %copy-start.2 = (f32[32,32,128]{2,1,0:T(8,128)S(1)}, f32[32,32,128]{2,1,0:T(8,128)}, u32[]{:S(2)}) copy-start(f32[32,32,128]{2,1,0:T(8,128)} %param.10) | copy-start | bytes 1572868
  0.7 9.2 %copy-start.4 = (f32[32,32,128]{2,1,0:T(8,128)S(1)}, f32[32,32,128]{2,1,0:T(8,128)}, u32[]{:S(2)}) copy-start(f32[32,32,128]{2,1,0:T(8,128)} %param.11) | copy-start | bytes 1572868
  11.5 13.5 %collective-permute-start.1 = (f32[2,32,32,6]{2,1,3,0:T(8,128)}, f32[2,32,32,6]{2,1,3,0:T(8,128)S(1)}, u32[]{:S(2)}, u32[]{:S(2)}) collective-permute-start(f32[2,32,32,6]{2,1,3,0:T(8,128)} %copy.26), channel_id=1, source_target_pairs={{4,0},{8,4},{12,8},{16,12},{20,16},{24,20},{28,24},{0,28},{5,1},{9... | collective-permute-start | bytes 147464 | tf_op jit(solution)/shard_map/ppermute | solution.py:36
  16.5 7.4 %copy-start.6 = (s32[32,128]{1,0:T(8,128)S(1)}, s32[32,128]{1,0:T(8,128)}, u32[]{:S(2)}) copy-start(s32[32,128]{1,0:T(8,128)} %param.13) | copy-start | bytes 49156
  16.5 7.4 %copy-start.7 = (s32[32,128]{1,0:T(8,128)S(1)}, s32[32,128]{1,0:T(8,128)}, u32[]{:S(2)}) copy-start(s32[32,128]{1,0:T(8,128)} %param.14) | copy-start | bytes 49156
  17.1 9.7 %collective-permute-start = (f32[2,32,32,6]{2,1,3,0:T(8,128)S(1)}, f32[2,32,32,6]{2,1,3,0:T(8,128)}, u32[]{:S(2)}, u32[]{:S(2)}) collective-permute-start(f32[2,32,32,6]{2,1,3,0:T(8,128)S(1)} %copy.25), channel_id=1, source_target_pairs={{0,4},{4,8},{8,12},{12,16},{16,20},{20,24},{24,28},{28,0},{1,5},{5... | collective-permute-start | bytes 147464 | tf_op jit(solution)/shard_map/ppermute | solution.py:34
  20.3 16.6 %all-to-all-start = ((bf16[4,2,16384]{2,1,0:T(2,128)(2,1)}), bf16[4,2,16384]{2,1,0:T(2,128)(2,1)S(1)}, u32[]{:S(2)}, u32[]{:S(2)}) async-start(bf16[4,2,16384]{2,1,0:T(2,128)(2,1)} %reshape.28), calls=%async_computation | async-start | bytes 524288 | tf_op jit(solution)/shard_map/all_to_all | solution.py:81
  45.5 2.8 %copy-start.5 = (f32[128,1024]{0,1:T(8,128)S(1)}, f32[128,1024]{0,1:T(8,128)}, u32[]{:S(2)}) copy-start(f32[128,1024]{0,1:T(8,128)} %copy.31) | copy-start | bytes 1572868
  48.2 6.8 %copy-start.3 = (f32[32,32,129]{2,1,0:T(8,128)S(1)}, f32[32,32,129]{2,1,0:T(8,128)}, u32[]{:S(2)}) copy-start(f32[32,32,129]{2,1,0:T(8,128)} %fusion.1) | copy-start | bytes 1585156
  51.6 9.4 %all-to-all-start.1 = ((bf16[4,2,16384]{2,1,0:T(2,128)(2,1)}), bf16[4,2,16384]{2,1,0:T(2,128)(2,1)S(1)}, u32[]{:S(2)}, u32[]{:S(2)}) async-start(bf16[4,2,16384]{2,1,0:T(2,128)(2,1)} %reshape.30), calls=%async_computation.1 | async-start | bytes 524288 | tf_op jit(solution)/shard_map/all_to_all | solution.py:93
where the time goes:
time: 64 us; the launch traced here: 63.5 us
  local copies, waits for them, and re-layouts  20.8 us (32%)
  other arithmetic  16.9 us (26%)
  starting transfers between devices  12.1 us (19%)
  blocking collectives  6.19 us (10%)
  waiting for transfers between devices  6.08 us (10%)
  between operations  0.96 us (2%)
    all_gather x1, blocking collectives, carried_in(): pieces = lax.all_gather(value, axis)  6.19 us
    ppermute x1, starting transfers between devices, with_halo(): lax.ppermute(head, axis, [((i + 1) % count, i) for i in range(count)])  5.03 us
    all_to_all x1, waiting for transfers between devices, shards(): lax.all_to_all(heat_cols, 'lev', split_axis=0, concat_axis=2, tiled=True)  4.71 us
    sub x6, other arithmetic, advance(): velocity[:, :, :-1] - courant * (pressure[:, :, 1:] - pressure[:, :, :-1])  4.45 us
    unnamed x20, local copies, waits for them, and re-layouts  4.37 us
    sub x6, other arithmetic, advance(): pressure[:, :, 1:-1] - courant * (velocity[:, :, 1:] - velocity[:, :, :-1])  4.32 us
    slice x3, local copies, waits for them, and re-layouts, combine_heating(): convect = jnp.sum(products[:schemes] * onehot[:, None, :, :], axis=0)  4.28 us
    all_to_all x1, starting transfers between devices, shards(): lax.all_to_all(local_theta, 'lev', split_axis=2, concat_axis=0, tiled=True)  3.59 us
  transfers between devices with their start and end apart: 4, of which 2 were waited for; matrix products, arithmetic and copies ran while one was open for 26% of the time, Pallas kernels for 0%

commit v1 on v0

v1 whole, which is shorter than its diff:
```python
import functools

import jax
import jax.numpy as jnp
import ml_dtypes
import numpy as np
from jax import lax
from jax.experimental import pallas as pl
from jax.experimental.pallas import tpu as pltpu
from jax.sharding import PartitionSpec as P

LEVELS = 128
SUBSTEPS = 6
SLOT = 16
CHUNK = 8
PACK = 16

courant = 0.9
F32 = jnp.float32
BF16 = jnp.bfloat16
MESH = pl.DeviceIdType.MESH


def substep_operator(width):
    halo = SUBSTEPS
    pad = 2 * halo
    pressure = np.zeros((2 * width, width + 2 * pad))
    velocity = np.zeros_like(pressure)
    cells = np.arange(width)
    pressure[cells, pad + cells] = 1.0
    velocity[width + cells, pad + cells] = 1.0
    for substep in range(SUBSTEPS):
        velocity = velocity - courant * (np.roll(pressure, -1, axis=1) - pressure)
        pressure = pressure - courant * (velocity - np.roll(velocity, 1, axis=1))
    spare = np.zeros((2 * width, width - 2 * halo))
    before, after = slice(pad - halo, pad), slice(pad + width, pad + width + halo)
    inside = slice(pad, pad + width)
    whole = np.concatenate(
        [
            pressure[:, inside], velocity[:, inside],
            pressure[:, before], velocity[:, before], spare,
            pressure[:, after], velocity[:, after], spare,
        ],
        axis=1,
    ).astype(np.float32)
    high = whole.astype(ml_dtypes.bfloat16)
    low = (whole - high.astype(np.float32)).astype(ml_dtypes.bfloat16)
    return high, low


def split(value):
    high = value.astype(BF16)
    return high, (value - high.astype(F32)).astype(BF16)


def dot(a, b):
    return jnp.dot(a, b, preferred_element_type=F32)


def kernel(
    dims,
    theta, thick, wind, surf, trig, clos, wts, mhi, mlo,
    p_out, v_out, h_out,
    theta_v, thick_v, wind_v, surf_v, trig_v, clos_v, w_v, mhi_v, mlo_v,
    gath, xh, xl, p_s, v_s, pack, pack_in, tot, tot_in, cpack, cpack_in, heat, hout,
    in_sem, out_sem, hout_sem, dir_send, dir_recv, par_send, par_recv,
    tot_send, tot_recv, halo_send, halo_recv, chalo_send, chalo_recv,
):
    levs, tiles, L, R, C, S = dims
    half = levs // 2
    chunks = R // CHUNK
    slots = C // SLOT
    srows = L * R // slots
    H = SUBSTEPS
    me = lax.axis_index("lev")
    here = lax.axis_index("tile")
    mate = me + 1 - 2 * (me % 2)
    right, left = (here + 1) % tiles, (here + tiles - 1) % tiles

    loads = [
        pltpu.make_async_copy(src, dst, in_sem.at[i])
        for i, (src, dst) in enumerate(
            [
                (theta, theta_v), (thick, thick_v), (surf, surf_v), (wind, wind_v), (mhi, mhi_v), (mlo, mlo_v),
                (wts.at[:, pl.ds(pl.multiple_of(me * L, 16), L), :], w_v), (trig, trig_v), (clos, clos_v),
            ]
        )
    ]
    for copy in loads:
        copy.start()
    barrier = pltpu.get_barrier_semaphore()
    for d in range(1, levs):
        pl.semaphore_signal(barrier, inc=1, device_id=(here, (me + d) % levs), device_id_type=MESH)
    for side in (left, right):
        pl.semaphore_signal(barrier, inc=1, device_id=(side, me), device_id_type=MESH)

    def slot_of(rank):
        return pl.ds(pl.multiple_of(rank * L, 16), L)

    def block_copy(owner, c, send, recv, target):
        block = gath.at[pl.ds(c * CHUNK, CHUNK), slot_of(owner), :]
        return pltpu.make_async_remote_copy(
            src_ref=block, dst_ref=block, send_sem=send, recv_sem=recv, device_id=(here, target), device_id_type=MESH
        )

    def direct(d, c):
        return block_copy(me, c, dir_send.at[d - 1, c], dir_recv.at[d - 1, c], (me + 2 * d) % levs)

    def to_mate(d, c):
        return block_copy((me + levs - 2 * d) % levs, c, par_send.at[d, c], par_recv.at[d, c], mate)

    def direct_in(d, c):
        return block_copy(
            (me + levs - 2 * d) % levs, c, dir_send.at[d - 1, c], dir_recv.at[d - 1, c], (me + 2 * d) % levs
        )

    def from_mate(d, c):
        return block_copy((mate + levs - 2 * d) % levs, c, par_send.at[d, c], par_recv.at[d, c], mate)

    loads[0].wait()
    for c in range(chunks):
        def relayout(i, _, c=c):
            r = c * CHUNK + i
            gath[r, slot_of(me), :] = theta_v[pl.ds(r, L, stride=R), :].astype(BF16)
            return 0

        lax.fori_loop(0, CHUNK, relayout, 0, unroll=True)
        if c == 0:
            pl.semaphore_wait(barrier, levs + 1)
        for d in range(1, half):
            direct(d, c).start()
        to_mate(0, c).start()

    for i in (1, 2, 3):
        loads[i].wait()

    def level(i, total):
        rows = pl.ds(pl.multiple_of((L - 1 - i) * R, R), R)
        thermal = theta_v[rows, :] * thick_v[rows, :] * LEVELS ** (-0.5)
        geopot = surf_v[...] + total + 0.5 * thermal
        xh[rows, 0:C], xl[rows, 0:C] = split(geopot)
        xh[rows, C : 2 * C], xl[rows, C : 2 * C] = split(wind_v[rows, :])
        return total + thermal

    tot[...] = lax.fori_loop(0, L, level, jnp.zeros((R, C), F32), unroll=4)

    def total_copy(d):
        return pltpu.make_async_remote_copy(
            src_ref=tot, dst_ref=tot_in.at[d - 1], send_sem=tot_send.at[d - 1], recv_sem=tot_recv.at[d - 1],
            device_id=(here, (me + d) % levs), device_id_type=MESH,
        )

    for d in range(1, levs):
        total_copy(d).start()

    loads[4].wait()
    loads[5].wait()
    per = 2
    for step in range(slots // per):
        rows = pl.ds(step * per * srows, per * srows)
        high, low = xh[rows, :], xl[rows, :]
        y = dot(high, mhi_v[...]) + dot(low, mhi_v[...]) + dot(high, mlo_v[...])
        p_s[rows, :] = y[:, 0:C]
        v_s[rows, :] = y[:, C : 2 * C]
        for j in range(per):
            g = step * per + j
            for side in range(2):
                part = y[j * srows : (j + 1) * srows, (2 + side) * C : (3 + side) * C]
                if g == 0:
                    pack[side] = part
                else:
                    pack[side] += pltpu.roll(part, g * SLOT, 1)

    def side_copy(src, dst, send, recv, side):
        return pltpu.make_async_remote_copy(
            src_ref=src.at[side], dst_ref=dst.at[side], send_sem=send.at[side], recv_sem=recv.at[side],
            device_id=((left, right)[side], me), device_id_type=MESH,
        )

    halos = [side_copy(pack, pack_in, halo_send, halo_recv, side) for side in range(2)]
    for copy in halos:
        copy.start()

    def forward(c):
        for d in range(1, half):
            direct_in(d, c).wait_recv()
            to_mate(d, c).start()

    carry = jnp.zeros((R, C), F32)
    for d in range(1, levs):
        total_copy(d).wait_recv()
        owner = (me + levs - d) % levs
        carry = carry + jnp.where(owner > me, tot_in[d - 1], 0.0)
    ch, cl = split(carry)
    yc = dot(ch, mhi_v[0:C, :]) + dot(cl, mhi_v[0:C, :]) + dot(ch, mlo_v[0:C, :])
    cpack[0] = yc[:, 2 * C : 3 * C]
    cpack[1] = yc[:, 3 * C : 4 * C]
    chalos = [side_copy(cpack, cpack_in, chalo_send, chalo_recv, side) for side in range(2)]
    for copy in chalos:
        copy.start()

    for i in (6, 7, 8):
        loads[i].wait()

    def physics(c):
        for d in range(half):
            from_mate(d, c).wait_recv()

        def pair(i, _):
            r = c * CHUNK + 2 * i
            cols = jnp.concatenate([gath[r], gath[r + 1]], axis=1)
            res = dot(w_v[...].reshape(S * L, levs * L), cols)
            for j in range(2):
                mine = res[:, j * C : (j + 1) * C]
                scheme = jnp.broadcast_to(clos_v[pl.ds(r + j, 1), :], (L, C))
                on = jnp.broadcast_to(trig_v[pl.ds(r + j, 1), :].astype(F32), (L, C))
                chosen = mine[0:L]
                for s in range(1, S - 1):
                    chosen = jnp.where(scheme == s, mine[s * L : (s + 1) * L], chosen)
                heat[pl.ds(r + j, L, stride=R), :] = mine[(S - 1) * L :] + on * chosen
            return 0

        lax.fori_loop(0, CHUNK // 2, pair, 0, unroll=True)

    houts = []

    def emit(o):
        def one(k, _):
            hout[k, pl.ds(o * PACK, PACK), :] = heat[pl.ds(pl.multiple_of(k * R + o * PACK, PACK), PACK), :].astype(BF16)
            return 0

        lax.fori_loop(0, L, one, 0, unroll=8)
        rows = pl.ds(o * PACK, PACK)
        copy = pltpu.make_async_copy(hout.at[:, rows, :], h_out.at[:, rows, :], hout_sem.at[o])
        copy.start()
        houts.append(copy)

    outs = []

    def finish():
        lane = lax.broadcasted_iota(jnp.int32, (R, C), 1)
        for side in range(2):
            halos[side].wait_recv()
            chalos[side].wait_recv()

        def edges(to_left, to_right, start, rows):
            at = lax.broadcasted_iota(jnp.int32, (rows, C), 1)
            first = pltpu.roll(to_right, (C - start) % C, 1)
            last = pltpu.roll(to_left, (2 * C - H - start) % C, 1)
            return jnp.where(at < H, first, jnp.where(at >= C - H, last, 0.0))

        p_c = yc[:, 0:C] + edges(cpack_in[0], cpack_in[1], 0, R)
        v_c = yc[:, C : 2 * C] + edges(cpack_in[0], cpack_in[1], H, R)
        for g in range(slots):
            rows = pl.ds(g * srows, srows)
            for field, (held, common) in enumerate(((p_s, p_c), (v_s, v_c))):
                fix = edges(pack_in[0], pack_in[1], g * SLOT + field * H, srows)
                many = held[rows, :] + fix
                held[rows, :] = (many.reshape(srows // R, R, C) + common[None]).reshape(srows, C)
                copy = pltpu.make_async_copy(
                    held.at[rows, :], (p_out, v_out)[field].at[rows, :], out_sem.at[field, g]
                )
                copy.start()
                outs.append(copy)

    per_pack = PACK // CHUNK
    for c in range(chunks):
        forward(c)
        if c == chunks - 1:
            finish()
        if c >= 1:
            physics(c - 1)
            if c % per_pack == 0:
                emit(c // per_pack - 1)
    physics(chunks - 1)
    emit(chunks // per_pack - 1)

    for c in range(chunks):
        for d in range(1, half):
            direct(d, c).wait_send()
        for d in range(half):
            to_mate(d, c).wait_send()
    for d in range(1, levs):
        total_copy(d).wait_send()
    for copy in halos + chalos:
        copy.wait_send()
    for copy in outs + houts:
        copy.wait()


def shards(levs, tiles, theta, thickness, wind, surface, trigger, closure, closure_weights):
    L, R, C = theta.shape
    S = closure_weights.shape[0]
    half = levs // 2
    chunks = R // CHUNK
    slots = C // SLOT
    srows = L * R // slots
    high, low = substep_operator(C)
    flat = (L * R, C)
    anywhere = pl.BlockSpec(memory_space=pl.ANY)
    vmem, dma = pltpu.VMEM, pltpu.SemaphoreType.DMA
    p, v, h = pl.pallas_call(
        functools.partial(kernel, (levs, tiles, L, R, C, S)),
        out_shape=(
            jax.ShapeDtypeStruct(flat, F32), jax.ShapeDtypeStruct(flat, F32), jax.ShapeDtypeStruct((L, R, C), BF16)
        ),
        in_specs=[anywhere] * 9,
        out_specs=(anywhere,) * 3,
        scratch_shapes=[
            vmem(flat, F32), vmem(flat, F32), vmem(flat, F32),
            vmem((R, C), F32), vmem((R, C), jnp.int32), vmem((R, C), jnp.int32),
            vmem((S, L, levs * L), BF16), vmem((2 * C, 4 * C), BF16), vmem((2 * C, 4 * C), BF16),
            vmem((R, levs * L, C), BF16),
            vmem((L * R, 2 * C), BF16), vmem((L * R, 2 * C), BF16),
            vmem(flat, F32), vmem(flat, F32),
            vmem((2, srows, C), F32), vmem((2, srows, C), F32),
            vmem((R, C), F32), vmem((levs - 1, R, C), F32),
            vmem((2, R, C), F32), vmem((2, R, C), F32),
            vmem(flat, F32), vmem((L, R, C), BF16),
            dma((9,)), dma((2, slots)), dma((R // PACK,)),
            dma((max(half - 1, 1), chunks)), dma((max(half - 1, 1), chunks)), dma((half, chunks)), dma((half, chunks)),
            dma((levs - 1,)), dma((levs - 1,)), dma((2,)), dma((2,)), dma((2,)), dma((2,)),
        ],
        compiler_params=pltpu.CompilerParams(
            collective_id=0, has_side_effects=True, vmem_limit_bytes=24 * 1024 * 1024
        ),
        cost_estimate=pl.CostEstimate(flops=10**9, bytes_accessed=4 * 10**6, transcendentals=0),
    )(
        theta.reshape(flat), thickness.reshape(flat), wind.reshape(flat), surface, trigger, closure, closure_weights,
        jnp.asarray(high), jnp.asarray(low),
    )
    return p.reshape(L, R, C), v.reshape(L, R, C), h


def solution(mesh):
    cells, sheet = P("lev", None, "tile"), P(None, "tile")
    return jax.shard_map(
        functools.partial(shards, mesh.shape["lev"], mesh.shape["tile"]),
        mesh=mesh,
        in_specs=(cells, cells, cells, sheet, sheet, sheet, P()),
        out_specs=(cells, cells, cells),
        check_vma=False,
    )
```

time: 64 us -> 33.2 us (0.52)
  Pallas kernels: 0 us -> 21.7 us
  other arithmetic: 16.9 us -> 0 us
  starting transfers between devices: 12.1 us -> 0 us
  local copies, waits for them, and re-layouts: 20.8 us -> 10.4 us
  blocking collectives: 6.19 us -> 0 us
  waiting for transfers between devices: 6.08 us -> 0 us
    pallas_call x0 -> x1, Pallas kernels: none -> 21.7 us  [shards(): pl.pallas_call(functools.partial(kernel, (levs, tiles, L, R, C, S)), out_...]
    sub x12 -> x0, other arithmetic: 8.77 us -> none  [the longest x6 4.45 us: advance(): velocity[:, :, :-1] - courant * (pressure[:, :, 1:] - pressure[:, :, :-1])]
    slice x7 -> x0, local copies, waits for them, and re-layouts: 7.12 us -> none  [the longest x3 4.28 us: combine_heating(): convect = jnp.sum(products[:schemes] * onehot[:, None, :, :], axis=0)]
    all_to_all x2 -> x0, starting transfers between devices: 6.99 us -> none  [the longest x1 3.59 us: shards(): lax.all_to_all(local_theta, 'lev', split_axis=2, concat_axis=0, tiled=True)]
    all_gather x1 -> x0, blocking collectives: 6.19 us -> none  [carried_in(): pieces = lax.all_gather(value, axis)]
    unnamed x20 -> x21, local copies, waits for them, and re-layouts: 4.37 us -> 10.4 us
    ppermute x2 -> x0, starting transfers between devices: 5.09 us -> none  [the longest x1 5.03 us: with_halo(): lax.ppermute(head, axis, [((i + 1) % count, i) for i in range(count)])]
    all_to_all x2 -> x0, waiting for transfers between devices: 4.71 us -> none  [the longest x1 4.71 us: shards(): lax.all_to_all(heat_cols, 'lev', split_axis=0, concat_axis=2, tiled=True)]
  transfers between devices with their start and end apart: 4 -> 0, of which waited for: 2 -> 0; matrix products, arithmetic and copies ran while one was open for 26% -> 0% of each run, Pallas kernels for 0% -> 0%
where the time goes in v1:
time: 33.2 us; the launch traced here: 32.7 us
  Pallas kernels  21.7 us (65%)
  local copies, waits for them, and re-layouts  10.4 us (31%)
  between operations  0.66 us (2%)
    pallas_call x1, Pallas kernels, shards(): pl.pallas_call(functools.partial(kernel, (levs, tiles, L, R, C, S)), out_...  21.7 us
    unnamed x21, local copies, waits for them, and re-layouts  10.4 us

profile of v1, /device:TPU:0, one launch (start us, length us, event | category | flops | bytes accessed | tf_op | source)
XLA Modules:
  0.0 32.7 jit_solution(1934177883864645825)
XLA Ops:
  0.6 0.0 copy-start
  0.6 1.0 %copy-done = f32[32,32,128]{2,1,0:T(8,128)S(1)} copy-done((f32[32,32,128]{2,1,0:T(8,128)S(1)}, f32[32,32,128]{2,1,0:T(8,128)}, u32[]{:S(2)}) %copy-start) | copy-done | bytes 524312
  1.7 0.0 copy-start.1
  1.7 1.0 %copy-done.1 = f32[32,32,128]{2,1,0:T(8,128)S(1)} copy-done((f32[32,32,128]{2,1,0:T(8,128)S(1)}, f32[32,32,128]{2,1,0:T(8,128)}, u32[]{:S(2)}) %copy-start.1) | copy-done | bytes 524312
  2.7 0.0 copy-start.2
  2.7 1.0 %copy-done.2 = f32[32,32,128]{2,1,0:T(8,128)S(1)} copy-done((f32[32,32,128]{2,1,0:T(8,128)S(1)}, f32[32,32,128]{2,1,0:T(8,128)}, u32[]{:S(2)}) %copy-start.2) | copy-done | bytes 524312
  3.8 0.0 copy-start.3
  3.8 0.9 %copy-done.3 = bf16[4,128,128]{2,1,0:T(8,128)(2,1)S(1)} copy-done((bf16[4,128,128]{2,1,0:T(8,128)(2,1)S(1)}, bf16[4,128,128]{2,1,0:T(8,128)(2,1)}, u32[]{:S(2)}) %copy-start.3) | copy-done | bytes 131096
  4.7 0.0 copy-start.4
  4.7 0.7 %copy-done.4 = f32[32,128]{1,0:T(8,128)S(1)} copy-done((f32[32,128]{1,0:T(8,128)S(1)}, f32[32,128]{1,0:T(8,128)}, u32[]{:S(2)}) %copy-start.4) | copy-done | bytes 16408
  5.4 0.0 copy-start.5
  5.4 0.7 %copy-done.5 = s32[32,128]{1,0:T(8,128)S(1)} copy-done((s32[32,128]{1,0:T(8,128)S(1)}, s32[32,128]{1,0:T(8,128)}, u32[]{:S(2)}) %copy-start.5) | copy-done | bytes 16408
  6.1 0.0 copy-start.6
  6.1 0.7 %copy-done.6 = s32[32,128]{1,0:T(8,128)S(1)} copy-done((s32[32,128]{1,0:T(8,128)S(1)}, s32[32,128]{1,0:T(8,128)}, u32[]{:S(2)}) %copy-start.6) | copy-done | bytes 16408
  6.8 0.0 copy-start.7
  6.8 0.9 %copy-done.7 = bf16[256,512]{1,0:T(8,128)(2,1)S(1)} copy-done((bf16[256,512]{1,0:T(8,128)(2,1)S(1)}, bf16[256,512]{1,0:T(8,128)(2,1)}, u32[]{:S(2)}) %copy-start.7) | copy-done | bytes 262168
  7.8 0.0 copy-start.8
  7.8 0.9 %copy-done.8 = bf16[256,512]{1,0:T(8,128)(2,1)S(1)} copy-done((bf16[256,512]{1,0:T(8,128)(2,1)S(1)}, bf16[256,512]{1,0:T(8,128)(2,1)}, u32[]{:S(2)}) %copy-start.8) | copy-done | bytes 262168
  8.7 21.7 %shard_map.112 = (f32[1024,128]{1,0:T(8,128)S(1)}, f32[1024,128]{1,0:T(8,128)S(1)}, bf16[32,32,128]{2,1,0:T(8,128)(2,1)S(1)}) custom-call(f32[1024,128]{1,0:T(8,128)S(1)} %bitcast.7, f32[1024,128]{1,0:T(8,128)S(1)} %bitcast.8, f32[1024,128]{1,0:T(8,128)S(1)} %bitcast.9, f32[32,128]{1,0:T(8,128)S(1)} %copy-done.4, s32[32,128]{1,0:T(8,128)S(1)} %copy-done.5, ...), custom_call_target="tpu_custom_call" | custom-call | flops 1000000000 | bytes 4000000 | tf_op jit(solution)/shard_map/pallas_call | solution.py:302
  30.4 0.8 %copy.15 = f32[32,32,128]{2,1,0:T(8,128)} copy(f32[32,32,128]{2,1,0:T(8,128)S(1)} %bitcast.6) | data formatting | bytes 1048576
  31.2 0.8 %copy.16 = f32[32,32,128]{2,1,0:T(8,128)} copy(f32[32,32,128]{2,1,0:T(8,128)S(1)} %bitcast.5) | data formatting | bytes 1048576
  32.0 0.7 %copy.17 = bf16[32,32,128]{2,1,0:T(8,128)(2,1)} copy(bf16[32,32,128]{2,1,0:T(8,128)(2,1)S(1)} %get-tuple-element.14) | data formatting | bytes 524288
Async XLA Ops:
  0.6 1.0 %copy-start = (f32[32,32,128]{2,1,0:T(8,128)S(1)}, f32[32,32,128]{2,1,0:T(8,128)}, u32[]{:S(2)}) copy-start(f32[32,32,128]{2,1,0:T(8,128)} %param.9) | copy-start | bytes 1572868
  1.7 1.0 %copy-start.1 = (f32[32,32,128]{2,1,0:T(8,128)S(1)}, f32[32,32,128]{2,1,0:T(8,128)}, u32[]{:S(2)}) copy-start(f32[32,32,128]{2,1,0:T(8,128)} %param.10) | copy-start | bytes 1572868
  2.7 1.0 %copy-start.2 = (f32[32,32,128]{2,1,0:T(8,128)S(1)}, f32[32,32,128]{2,1,0:T(8,128)}, u32[]{:S(2)}) copy-start(f32[32,32,128]{2,1,0:T(8,128)} %param.11) | copy-start | bytes 1572868
  3.8 0.9 %copy-start.3 = (bf16[4,128,128]{2,1,0:T(8,128)(2,1)S(1)}, bf16[4,128,128]{2,1,0:T(8,128)(2,1)}, u32[]{:S(2)}) copy-start(bf16[4,128,128]{2,1,0:T(8,128)(2,1)} %wts.1) | copy-start | bytes 393220
  4.7 0.7 %copy-start.4 = (f32[32,128]{1,0:T(8,128)S(1)}, f32[32,128]{1,0:T(8,128)}, u32[]{:S(2)}) copy-start(f32[32,128]{1,0:T(8,128)} %surf.1) | copy-start | bytes 49156
  5.4 0.7 %copy-start.5 = (s32[32,128]{1,0:T(8,128)S(1)}, s32[32,128]{1,0:T(8,128)}, u32[]{:S(2)}) copy-start(s32[32,128]{1,0:T(8,128)} %trig.1) | copy-start | bytes 49156
  6.1 0.7 %copy-start.6 = (s32[32,128]{1,0:T(8,128)S(1)}, s32[32,128]{1,0:T(8,128)}, u32[]{:S(2)}) copy-start(s32[32,128]{1,0:T(8,128)} %clos.1) | copy-start | bytes 49156
  6.8 0.9 %copy-start.7 = (bf16[256,512]{1,0:T(8,128)(2,1)S(1)}, bf16[256,512]{1,0:T(8,128)(2,1)}, u32[]{:S(2)}) copy-start(bf16[256,512]{1,0:T(8,128)(2,1)} %constant.5.clone.mlo) | copy-start | bytes 786436
  7.8 0.9 %copy-start.8 = (bf16[256,512]{1,0:T(8,128)(2,1)S(1)}, bf16[256,512]{1,0:T(8,128)(2,1)}, u32[]{:S(2)}) copy-start(bf16[256,512]{1,0:T(8,128)(2,1)} %constant.4.clone.mhi) | copy-start | bytes 786436

commit v2 on v1

--- a/solution.py
+++ b/solution.py
@@ -2,7 +2,6 @@
 
 import jax
 import jax.numpy as jnp
-import ml_dtypes
 import numpy as np
 from jax import lax
 from jax.experimental import pallas as pl
@@ -42,10 +41,8 @@
             pressure[:, after], velocity[:, after], spare,
         ],
         axis=1,
-    ).astype(np.float32)
-    high = whole.astype(ml_dtypes.bfloat16)
-    low = (whole - high.astype(np.float32)).astype(ml_dtypes.bfloat16)
-    return high, low
+    )
+    return whole.astype(np.float32)
 
 
 def split(value):
@@ -59,11 +56,11 @@
 
 def kernel(
     dims,
-    theta, thick, wind, surf, trig, clos, wts, mhi, mlo,
-    p_out, v_out, h_out,
-    theta_v, thick_v, wind_v, surf_v, trig_v, clos_v, w_v, mhi_v, mlo_v,
-    gath, xh, xl, p_s, v_s, pack, pack_in, tot, tot_in, cpack, cpack_in, heat, hout,
-    in_sem, out_sem, hout_sem, dir_send, dir_recv, par_send, par_recv,
+    theta, thick, wind, surf, trig, clos, wts, operator,
+    p_s, v_s, hout,
+    theta_v, thick_v, wind_v, surf_v, trig_v, clos_v, w_v, op_v, mhi_v, mlo_v,
+    gath, xh, xl, pack, pack_in, tot, tot_in, cpack, cpack_in, heat,
+    in_sem, dir_send, dir_recv, par_send, par_recv,
     tot_send, tot_recv, halo_send, halo_recv, chalo_send, chalo_recv,
 ):
     levs, tiles, L, R, C, S = dims
@@ -81,7 +78,7 @@
         pltpu.make_async_copy(src, dst, in_sem.at[i])
         for i, (src, dst) in enumerate(
             [
-                (theta, theta_v), (thick, thick_v), (surf, surf_v), (wind, wind_v), (mhi, mhi_v), (mlo, mlo_v),
+                (theta, theta_v), (thick, thick_v), (surf, surf_v), (wind, wind_v), (operator, op_v),
                 (wts.at[:, pl.ds(pl.multiple_of(me * L, 16), L), :], w_v), (trig, trig_v), (clos, clos_v),
             ]
         )
@@ -154,7 +151,7 @@
         total_copy(d).start()
 
     loads[4].wait()
-    loads[5].wait()
+    mhi_v[...], mlo_v[...] = split(op_v[...])
     per = 2
     for step in range(slots // per):
         rows = pl.ds(step * per * srows, per * srows)
@@ -199,7 +196,7 @@
     for copy in chalos:
         copy.start()
 
-    for i in (6, 7, 8):
+    for i in (5, 6, 7):
         loads[i].wait()
 
     def physics(c):
@@ -222,20 +219,12 @@
 
         lax.fori_loop(0, CHUNK // 2, pair, 0, unroll=True)
 
-    houts = []
-
     def emit(o):
         def one(k, _):
             hout[k, pl.ds(o * PACK, PACK), :] = heat[pl.ds(pl.multiple_of(k * R + o * PACK, PACK), PACK), :].astype(BF16)
             return 0
 
         lax.fori_loop(0, L, one, 0, unroll=8)
-        rows = pl.ds(o * PACK, PACK)
-        copy = pltpu.make_async_copy(hout.at[:, rows, :], h_out.at[:, rows, :], hout_sem.at[o])
-        copy.start()
-        houts.append(copy)
-
-    outs = []
 
     def finish():
         lane = lax.broadcasted_iota(jnp.int32, (R, C), 1)
@@ -257,21 +246,16 @@
                 fix = edges(pack_in[0], pack_in[1], g * SLOT + field * H, srows)
                 many = held[rows, :] + fix
                 held[rows, :] = (many.reshape(srows // R, R, C) + common[None]).reshape(srows, C)
-                copy = pltpu.make_async_copy(
-                    held.at[rows, :], (p_out, v_out)[field].at[rows, :], out_sem.at[field, g]
-                )
-                copy.start()
-                outs.append(copy)
 
     per_pack = PACK // CHUNK
     for c in range(chunks):
         forward(c)
-        if c == chunks - 1:
-            finish()
         if c >= 1:
             physics(c - 1)
             if c % per_pack == 0:
                 emit(c // per_pack - 1)
+        if c == chunks - 2:
+            finish()
     physics(chunks - 1)
     emit(chunks // per_pack - 1)
 
@@ -284,7 +268,15 @@
         total_copy(d).wait_send()
     for copy in halos + chalos:
         copy.wait_send()
-    for copy in outs + houts:
+
+
+def store_kernel(p, v, h, p_out, v_out, h_out, sem):
+    copies = [
+        pltpu.make_async_copy(src, dst, sem.at[i]) for i, (src, dst) in enumerate(((p, p_out), (v, v_out), (h, h_out)))
+    ]
+    for copy in copies:
+        copy.start()
+    for copy in copies:
         copy.wait()
 
 
@@ -295,29 +287,27 @@
     chunks = R // CHUNK
     slots = C // SLOT
     srows = L * R // slots
-    high, low = substep_operator(C)
     flat = (L * R, C)
-    anywhere = pl.BlockSpec(memory_space=pl.ANY)
+    hbm = pl.BlockSpec(memory_space=pltpu.HBM)
     vmem, dma = pltpu.VMEM, pltpu.SemaphoreType.DMA
     p, v, h = pl.pallas_call(
         functools.partial(kernel, (levs, tiles, L, R, C, S)),
         out_shape=(
             jax.ShapeDtypeStruct(flat, F32), jax.ShapeDtypeStruct(flat, F32), jax.ShapeDtypeStruct((L, R, C), BF16)
         ),
-        in_specs=[anywhere] * 9,
-        out_specs=(anywhere,) * 3,
+        in_specs=[hbm] * 8,
+        out_specs=(pl.BlockSpec(memory_space=pltpu.VMEM),) * 3,
         scratch_shapes=[
             vmem(flat, F32), vmem(flat, F32), vmem(flat, F32),
             vmem((R, C), F32), vmem((R, C), jnp.int32), vmem((R, C), jnp.int32),
-            vmem((S, L, levs * L), BF16), vmem((2 * C, 4 * C), BF16), vmem((2 * C, 4 * C), BF16),
+            vmem((S, L, levs * L), BF16), vmem((2 * C, 4 * C), F32), vmem((2 * C, 4 * C), BF16), vmem((2 * C, 4 * C), BF16),
             vmem((R, levs * L, C), BF16),
             vmem((L * R, 2 * C), BF16), vmem((L * R, 2 * C), BF16),
-            vmem(flat, F32), vmem(flat, F32),
             vmem((2, srows, C), F32), vmem((2, srows, C), F32),
             vmem((R, C), F32), vmem((levs - 1, R, C), F32),
             vmem((2, R, C), F32), vmem((2, R, C), F32),
-            vmem(flat, F32), vmem((L, R, C), BF16),
-            dma((9,)), dma((2, slots)), dma((R // PACK,)),
+            vmem(flat, F32),
+            dma((8,)),
             dma((max(half - 1, 1), chunks)), dma((max(half - 1, 1), chunks)), dma((half, chunks)), dma((half, chunks)),
             dma((levs - 1,)), dma((levs - 1,)), dma((2,)), dma((2,)), dma((2,)), dma((2,)),
         ],
@@ -326,9 +316,21 @@
         ),
         cost_estimate=pl.CostEstimate(flops=10**9, bytes_accessed=4 * 10**6, transcendentals=0),
     )(
-        theta.reshape(flat), thickness.reshape(flat), wind.reshape(flat), surface, trigger, closure, closure_weights,
-        jnp.asarray(high), jnp.asarray(low),
+        *(
+            pltpu.with_memory_space_constraint(value, pltpu.HBM)
+            for value in (
+                theta.reshape(flat), thickness.reshape(flat), wind.reshape(flat), surface, trigger, closure,
+                closure_weights, jnp.asarray(substep_operator(C)),
+            )
+        )
     )
+    p, v, h = pl.pallas_call(
+        store_kernel,
+        out_shape=tuple(jax.ShapeDtypeStruct(a.shape, a.dtype) for a in (p, v, h)),
+        in_specs=[pl.BlockSpec(memory_space=pltpu.VMEM)] * 3,
+        out_specs=(hbm,) * 3,
+        scratch_shapes=[dma((3,))],
+    )(p, v, h)
     return p.reshape(L, R, C), v.reshape(L, R, C), h
 
 

time: 33.2 us -> 24.9 us (0.75)
  local copies, waits for them, and re-layouts: 10.4 us -> 2.28 us
    unnamed x21 -> x6, local copies, waits for them, and re-layouts: 10.4 us -> 2.28 us
    pallas_call x1, Pallas kernels: 21.7 us -> 19.3 us  [shards(): pl.pallas_call(functools.partial(kernel, (levs, tiles, L, R, C, S)), out_...]
    pallas_call x0 -> x1, Pallas kernels: none -> 2.34 us  [shards(): pl.pallas_call(store_kernel, out_shape=tuple((jax.ShapeDtypeStruct(a.shap...]
where the time goes in v2:
time: 24.9 us; the launch traced here: 24.6 us
  Pallas kernels  21.6 us (87%)
  local copies, waits for them, and re-layouts  2.28 us (9%)
  between operations  0.65 us (3%)
    pallas_call x1, Pallas kernels, shards(): pl.pallas_call(functools.partial(kernel, (levs, tiles, L, R, C, S)), out_...  19.3 us
    pallas_call x1, Pallas kernels, shards(): pl.pallas_call(store_kernel, out_shape=tuple((jax.ShapeDtypeStruct(a.shap...  2.34 us
    unnamed x6, local copies, waits for them, and re-layouts  2.28 us

profile of v2, /device:TPU:0, one launch (start us, length us, event | category | flops | bytes accessed | tf_op | source)
XLA Modules:
  0.0 24.6 jit_solution(7592979882061502292)
XLA Ops:
  0.6 19.3 %shard_map.103 = (f32[1024,128]{1,0:T(8,128)S(1)}, f32[1024,128]{1,0:T(8,128)S(1)}, bf16[32,32,128]{2,1,0:T(8,128)(2,1)S(1)}) custom-call(f32[1024,128]{1,0:T(8,128)} %bitcast.5, f32[1024,128]{1,0:T(8,128)} %bitcast.6, f32[1024,128]{1,0:T(8,128)} %bitcast.7, f32[32,128]{1,0:T(8,128)} %surf.1, s32[32,128]{1,0:T(8,128)} %trig.1, s32[32,128]{1,0:T(8,128)} %clos.1, ...), custom_call_target="tpu_custom_call" | custom-call | flops 1000000000 | bytes 4000000 | tf_op jit(solution)/shard_map/pallas_call | solution.py:293
  19.9 0.0 copy-start
  19.9 0.8 %copy-done = f32[1024,128]{1,0:T(8,128)} copy-done((f32[1024,128]{1,0:T(8,128)}, f32[1024,128]{1,0:T(8,128)S(1)}, u32[]{:S(2)}) %copy-start) | copy-done | bytes 524312
  20.7 0.0 copy-start.1
  20.7 0.8 %copy-done.1 = f32[1024,128]{1,0:T(8,128)} copy-done((f32[1024,128]{1,0:T(8,128)}, f32[1024,128]{1,0:T(8,128)S(1)}, u32[]{:S(2)}) %copy-start.1) | copy-done | bytes 524312
  21.5 0.0 copy-start.2
  21.5 0.7 %copy-done.2 = bf16[32,32,128]{2,1,0:T(8,128)(2,1)} copy-done((bf16[32,32,128]{2,1,0:T(8,128)(2,1)}, bf16[32,32,128]{2,1,0:T(8,128)(2,1)S(1)}, u32[]{:S(2)}) %copy-start.2) | copy-done | bytes 262168
  22.2 2.3 %shard_map.104 = (f32[1024,128]{1,0:T(8,128)}, f32[1024,128]{1,0:T(8,128)}, bf16[32,32,128]{2,1,0:T(8,128)(2,1)}) custom-call(f32[1024,128]{1,0:T(8,128)} %copy-done, f32[1024,128]{1,0:T(8,128)} %copy-done.1, bf16[32,32,128]{2,1,0:T(8,128)(2,1)} %copy-done.2), custom_call_target="tpu_custom_call" | custom-call | tf_op jit(solution)/shard_map/pallas_call | solution.py:327
Async XLA Ops:
  19.9 0.8 %copy-start = (f32[1024,128]{1,0:T(8,128)}, f32[1024,128]{1,0:T(8,128)S(1)}, u32[]{:S(2)}) copy-start(f32[1024,128]{1,0:T(8,128)S(1)} %get-tuple-element.9.p) | copy-start | bytes 1572868
  20.7 0.8 %copy-start.1 = (f32[1024,128]{1,0:T(8,128)}, f32[1024,128]{1,0:T(8,128)S(1)}, u32[]{:S(2)}) copy-start(f32[1024,128]{1,0:T(8,128)S(1)} %get-tuple-element.10.v) | copy-start | bytes 1572868
  21.5 0.7 %copy-start.2 = (bf16[32,32,128]{2,1,0:T(8,128)(2,1)}, bf16[32,32,128]{2,1,0:T(8,128)(2,1)S(1)}, u32[]{:S(2)}) copy-start(bf16[32,32,128]{2,1,0:T(8,128)(2,1)S(1)} %get-tuple-element.11.h) | copy-start | bytes 786436

commit v3 on v2

--- a/solution.py
+++ b/solution.py
@@ -57,9 +57,9 @@
 def kernel(
     dims,
     theta, thick, wind, surf, trig, clos, wts, operator,
-    p_s, v_s, hout,
+    p_s, v_s, heat, pack_in, cmain, cpack_in,
     theta_v, thick_v, wind_v, surf_v, trig_v, clos_v, w_v, op_v, mhi_v, mlo_v,
-    gath, xh, xl, pack, pack_in, tot, tot_in, cpack, cpack_in, heat,
+    gath, xh, xl, pack, tot, tot_in, cpack,
     in_sem, dir_send, dir_recv, par_send, par_recv,
     tot_send, tot_recv, halo_send, halo_recv, chalo_send, chalo_recv,
 ):
@@ -190,6 +190,8 @@
         carry = carry + jnp.where(owner > me, tot_in[d - 1], 0.0)
     ch, cl = split(carry)
     yc = dot(ch, mhi_v[0:C, :]) + dot(cl, mhi_v[0:C, :]) + dot(ch, mlo_v[0:C, :])
+    cmain[0] = yc[:, 0:C]
+    cmain[1] = yc[:, C : 2 * C]
     cpack[0] = yc[:, 2 * C : 3 * C]
     cpack[1] = yc[:, 3 * C : 4 * C]
     chalos = [side_copy(cpack, cpack_in, chalo_send, chalo_recv, side) for side in range(2)]
@@ -219,46 +221,14 @@
 
         lax.fori_loop(0, CHUNK // 2, pair, 0, unroll=True)
 
-    def emit(o):
-        def one(k, _):
-            hout[k, pl.ds(o * PACK, PACK), :] = heat[pl.ds(pl.multiple_of(k * R + o * PACK, PACK), PACK), :].astype(BF16)
-            return 0
-
-        lax.fori_loop(0, L, one, 0, unroll=8)
-
-    def finish():
-        lane = lax.broadcasted_iota(jnp.int32, (R, C), 1)
-        for side in range(2):
-            halos[side].wait_recv()
-            chalos[side].wait_recv()
-
-        def edges(to_left, to_right, start, rows):
-            at = lax.broadcasted_iota(jnp.int32, (rows, C), 1)
-            first = pltpu.roll(to_right, (C - start) % C, 1)
-            last = pltpu.roll(to_left, (2 * C - H - start) % C, 1)
-            return jnp.where(at < H, first, jnp.where(at >= C - H, last, 0.0))
-
-        p_c = yc[:, 0:C] + edges(cpack_in[0], cpack_in[1], 0, R)
-        v_c = yc[:, C : 2 * C] + edges(cpack_in[0], cpack_in[1], H, R)
-        for g in range(slots):
-            rows = pl.ds(g * srows, srows)
-            for field, (held, common) in enumerate(((p_s, p_c), (v_s, v_c))):
-                fix = edges(pack_in[0], pack_in[1], g * SLOT + field * H, srows)
-                many = held[rows, :] + fix
-                held[rows, :] = (many.reshape(srows // R, R, C) + common[None]).reshape(srows, C)
-
-    per_pack = PACK // CHUNK
     for c in range(chunks):
         forward(c)
         if c >= 1:
             physics(c - 1)
-            if c % per_pack == 0:
-                emit(c // per_pack - 1)
-        if c == chunks - 2:
-            finish()
     physics(chunks - 1)
-    emit(chunks // per_pack - 1)
-
+
+    for copy in halos + chalos:
+        copy.wait_recv()
     for c in range(chunks):
         for d in range(1, half):
             direct(d, c).wait_send()
@@ -270,12 +240,43 @@
         copy.wait_send()
 
 
-def store_kernel(p, v, h, p_out, v_out, h_out, sem):
-    copies = [
-        pltpu.make_async_copy(src, dst, sem.at[i]) for i, (src, dst) in enumerate(((p, p_out), (v, v_out), (h, h_out)))
-    ]
-    for copy in copies:
+def finish_kernel(p_s, v_s, heat, pack, cmain, cpack, p_out, v_out, h_out, done, hout, out_sem, hout_sem):
+    L, R, C = hout.shape
+    slots = C // SLOT
+    srows = L * R // slots
+    H = SUBSTEPS
+    copies = []
+
+    def emit(o):
+        rows = pl.ds(o * PACK, PACK)
+
+        def one(k, _):
+            hout[k, rows, :] = heat[pl.ds(pl.multiple_of(k * R + o * PACK, PACK), PACK), :].astype(BF16)
+            return 0
+
+        lax.fori_loop(0, L, one, 0, unroll=8)
+        copy = pltpu.make_async_copy(hout.at[:, rows, :], h_out.at[:, rows, :], hout_sem.at[o])
         copy.start()
+        copies.append(copy)
+
+    def edges(to_left, to_right, start, rows):
+        at = lax.broadcasted_iota(jnp.int32, (rows, C), 1)
+        first = pltpu.roll(to_right, (C - start) % C, 1)
+        last = pltpu.roll(to_left, (2 * C - H - start) % C, 1)
+        return jnp.where(at < H, first, jnp.where(at >= C - H, last, 0.0))
+
+    for o in range(R // PACK):
+        emit(o)
+    common = [cmain[field] + edges(cpack[0], cpack[1], field * H, R) for field in range(2)]
+    for g in range(slots):
+        rows = pl.ds(g * srows, srows)
+        for field, (held, out) in enumerate(((p_s, p_out), (v_s, v_out))):
+            fix = edges(pack[0], pack[1], g * SLOT + field * H, srows)
+            many = (held[rows, :] + fix).reshape(srows // R, R, C) + common[field][None]
+            done[field, rows, :] = many.reshape(srows, C)
+            copy = pltpu.make_async_copy(done.at[field, rows, :], out.at[rows, :], out_sem.at[field, g])
+            copy.start()
+            copies.append(copy)
     for copy in copies:
         copy.wait()
 
@@ -288,25 +289,26 @@
     slots = C // SLOT
     srows = L * R // slots
     flat = (L * R, C)
+    near = pl.BlockSpec(memory_space=pltpu.VMEM)
     hbm = pl.BlockSpec(memory_space=pltpu.HBM)
     vmem, dma = pltpu.VMEM, pltpu.SemaphoreType.DMA
-    p, v, h = pl.pallas_call(
+    parts = pl.pallas_call(
         functools.partial(kernel, (levs, tiles, L, R, C, S)),
         out_shape=(
-            jax.ShapeDtypeStruct(flat, F32), jax.ShapeDtypeStruct(flat, F32), jax.ShapeDtypeStruct((L, R, C), BF16)
+            vmem(flat, F32), vmem(flat, F32), vmem(flat, F32),
+            vmem((2, srows, C), F32), vmem((2, R, C), F32), vmem((2, R, C), F32),
         ),
         in_specs=[hbm] * 8,
-        out_specs=(pl.BlockSpec(memory_space=pltpu.VMEM),) * 3,
+        out_specs=(near,) * 6,
         scratch_shapes=[
             vmem(flat, F32), vmem(flat, F32), vmem(flat, F32),
             vmem((R, C), F32), vmem((R, C), jnp.int32), vmem((R, C), jnp.int32),
             vmem((S, L, levs * L), BF16), vmem((2 * C, 4 * C), F32), vmem((2 * C, 4 * C), BF16), vmem((2 * C, 4 * C), BF16),
             vmem((R, levs * L, C), BF16),
             vmem((L * R, 2 * C), BF16), vmem((L * R, 2 * C), BF16),
-            vmem((2, srows, C), F32), vmem((2, srows, C), F32),
+            vmem((2, srows, C), F32),
             vmem((R, C), F32), vmem((levs - 1, R, C), F32),
-            vmem((2, R, C), F32), vmem((2, R, C), F32),
-            vmem(flat, F32),
+            vmem((2, R, C), F32),
             dma((8,)),
             dma((max(half - 1, 1), chunks)), dma((max(half - 1, 1), chunks)), dma((half, chunks)), dma((half, chunks)),
             dma((levs - 1,)), dma((levs - 1,)), dma((2,)), dma((2,)), dma((2,)), dma((2,)),
@@ -325,12 +327,18 @@
         )
     )
     p, v, h = pl.pallas_call(
-        store_kernel,
-        out_shape=tuple(jax.ShapeDtypeStruct(a.shape, a.dtype) for a in (p, v, h)),
-        in_specs=[pl.BlockSpec(memory_space=pltpu.VMEM)] * 3,
+        finish_kernel,
+        out_shape=(
+            jax.ShapeDtypeStruct(flat, F32), jax.ShapeDtypeStruct(flat, F32), jax.ShapeDtypeStruct((L, R, C), BF16)
+        ),
+        in_specs=[near] * 6,
         out_specs=(hbm,) * 3,
-        scratch_shapes=[dma((3,))],
-    )(p, v, h)
+        scratch_shapes=[
+            vmem((2,) + flat, F32), vmem((L, R, C), BF16), dma((2, slots)), dma((R // PACK,)),
+        ],
+        compiler_params=pltpu.CompilerParams(vmem_limit_bytes=16 * 1024 * 1024),
+        cost_estimate=pl.CostEstimate(flops=10**6, bytes_accessed=3 * 10**6, transcendentals=0),
+    )(*(pltpu.with_memory_space_constraint(part, pltpu.VMEM) for part in parts))
     return p.reshape(L, R, C), v.reshape(L, R, C), h
 
 

time: 24.9 us -> 20 us (0.80)
  Pallas kernels: 21.6 us -> 19.3 us
  local copies, waits for them, and re-layouts: 2.28 us -> 0 us
    unnamed x6 -> x0, local copies, waits for them, and re-layouts: 2.28 us -> none
    pallas_call x1, Pallas kernels: 19.3 us -> 17.8 us  [shards(): pl.pallas_call(functools.partial(kernel, (levs, tiles, L, R, C, S)), out_...]
    pallas_call x1, Pallas kernels: 2.34 us -> 1.45 us  [shards(): pl.pallas_call(finish_kernel, out_shape=(jax.ShapeDtypeStruct(flat, F32),...]
where the time goes in v3:
time: 20 us; the launch traced here: 19.9 us
  Pallas kernels  19.3 us (96%)
  between operations  0.64 us (3%)
    pallas_call x1, Pallas kernels, shards(): pl.pallas_call(functools.partial(kernel, (levs, tiles, L, R, C, S)), out_...  17.8 us
    pallas_call x1, Pallas kernels, shards(): pl.pallas_call(finish_kernel, out_shape=(jax.ShapeDtypeStruct(flat, F32),...  1.45 us

profile of v3, /device:TPU:0, one launch (start us, length us, event | category | flops | bytes accessed | tf_op | source)
XLA Modules:
  0.0 19.9 jit_solution(11964083539652999332)
XLA Ops:
  0.6 17.8 %shard_map.103 = (f32[1024,128]{1,0:T(8,128)S(1)}, f32[1024,128]{1,0:T(8,128)S(1)}, f32[1024,128]{1,0:T(8,128)S(1)}, f32[2,128,128]{2,1,0:T(8,128)S(1)}, f32[2,3...) custom-call(f32[1024,128]{1,0:T(8,128)} %bitcast.5, f32[1024,128]{1,0:T(8,128)} %bitcast.6, f32[1024,128]{1,0:T(8,128)} %bitcast.7, ...), custom_call_target="tpu_custom_call" | custom-call | flops 1000000000 | bytes 4000000 | tf_op jit(solution)/shard_map/pallas_call | solution.py:295
  18.4 1.5 %shard_map.104 = (f32[1024,128]{1,0:T(8,128)}, f32[1024,128]{1,0:T(8,128)}, bf16[32,32,128]{2,1,0:T(8,128)(2,1)}) custom-call(f32[1024,128]{1,0:T(8,128)S(1)} %get-tuple-element.12.p_s, f32[1024,128]{1,0:T(8,128)S(1)} %get-tuple-element.13.v_s, f32[1024,128]{1,0:T(8,128)S(1)} %get-tuple-element.14.heat, f32[2,128,128]{2,1,0:T(8,128)S(1)} %get-tuple-element.15.pack, ...), custom_call_target="tpu_custom_call" | custom-call | flops 1000000 | bytes 3000000 | tf_op jit(solution)/shard_map/pallas_call | solution.py:329

commit v4 on v3

--- a/solution.py
+++ b/solution.py
@@ -59,9 +59,9 @@
     theta, thick, wind, surf, trig, clos, wts, operator,
     p_s, v_s, heat, pack_in, cmain, cpack_in,
     theta_v, thick_v, wind_v, surf_v, trig_v, clos_v, w_v, op_v, mhi_v, mlo_v,
-    gath, xh, xl, pack, tot, tot_in, cpack,
+    gath, xh, xl, pack, tot, cpack,
     in_sem, dir_send, dir_recv, par_send, par_recv,
-    tot_send, tot_recv, halo_send, halo_recv, chalo_send, chalo_recv,
+    tot_send, tot_recv, totm_send, totm_recv, halo_send, halo_recv, chalo_send, chalo_recv,
 ):
     levs, tiles, L, R, C, S = dims
     half = levs // 2
@@ -114,7 +114,29 @@
     def from_mate(d, c):
         return block_copy((mate + levs - 2 * d) % levs, c, par_send.at[d, c], par_recv.at[d, c], mate)
 
+    def total_copy(owner, send, recv, target):
+        return pltpu.make_async_remote_copy(
+            src_ref=tot.at[owner], dst_ref=tot.at[owner], send_sem=send, recv_sem=recv,
+            device_id=(here, target), device_id_type=MESH,
+        )
+
+    def total_direct(d, inward=False):
+        owner = (me + levs - 2 * d) % levs if inward else me
+        return total_copy(owner, tot_send.at[d - 1], tot_recv.at[d - 1], (me + 2 * d) % levs)
+
+    def total_mate(d, inward=False):
+        owner = ((mate if inward else me) + levs - 2 * d) % levs
+        return total_copy(owner, totm_send.at[d], totm_recv.at[d], mate)
+
     loads[0].wait()
+    loads[1].wait()
+
+    def column(i, total):
+        rows = pl.ds(pl.multiple_of((L - 1 - i) * R, R), R)
+        return total + theta_v[rows, :] * thick_v[rows, :] * LEVELS ** (-0.5)
+
+    tot[me] = lax.fori_loop(0, L, column, jnp.zeros((R, C), F32), unroll=8)
+
     for c in range(chunks):
         def relayout(i, _, c=c):
             r = c * CHUNK + i
@@ -124,11 +146,14 @@
         lax.fori_loop(0, CHUNK, relayout, 0, unroll=True)
         if c == 0:
             pl.semaphore_wait(barrier, levs + 1)
+            for d in range(1, half):
+                total_direct(d).start()
+            total_mate(0).start()
         for d in range(1, half):
             direct(d, c).start()
         to_mate(0, c).start()
 
-    for i in (1, 2, 3):
+    for i in (2, 3):
         loads[i].wait()
 
     def level(i, total):
@@ -139,21 +164,16 @@
         xh[rows, C : 2 * C], xl[rows, C : 2 * C] = split(wind_v[rows, :])
         return total + thermal
 
-    tot[...] = lax.fori_loop(0, L, level, jnp.zeros((R, C), F32), unroll=4)
-
-    def total_copy(d):
-        return pltpu.make_async_remote_copy(
-            src_ref=tot, dst_ref=tot_in.at[d - 1], send_sem=tot_send.at[d - 1], recv_sem=tot_recv.at[d - 1],
-            device_id=(here, (me + d) % levs), device_id_type=MESH,
-        )
-
-    for d in range(1, levs):
-        total_copy(d).start()
+    lax.fori_loop(0, L, level, jnp.zeros((R, C), F32), unroll=4)
 
     loads[4].wait()
     mhi_v[...], mlo_v[...] = split(op_v[...])
     per = 2
     for step in range(slots // per):
+        if step == slots // per // 2:
+            for d in range(1, half):
+                total_direct(d, True).wait_recv()
+                total_mate(d).start()
         rows = pl.ds(step * per * srows, per * srows)
         high, low = xh[rows, :], xl[rows, :]
         y = dot(high, mhi_v[...]) + dot(low, mhi_v[...]) + dot(high, mlo_v[...])
@@ -183,11 +203,12 @@
             direct_in(d, c).wait_recv()
             to_mate(d, c).start()
 
+    forward(0)
+    for d in range(half):
+        total_mate(d, True).wait_recv()
     carry = jnp.zeros((R, C), F32)
-    for d in range(1, levs):
-        total_copy(d).wait_recv()
-        owner = (me + levs - d) % levs
-        carry = carry + jnp.where(owner > me, tot_in[d - 1], 0.0)
+    for owner in range(levs):
+        carry = carry + jnp.where(owner > me, tot[owner], 0.0)
     ch, cl = split(carry)
     yc = dot(ch, mhi_v[0:C, :]) + dot(cl, mhi_v[0:C, :]) + dot(ch, mlo_v[0:C, :])
     cmain[0] = yc[:, 0:C]
@@ -221,10 +242,9 @@
 
         lax.fori_loop(0, CHUNK // 2, pair, 0, unroll=True)
 
-    for c in range(chunks):
+    for c in range(1, chunks):
         forward(c)
-        if c >= 1:
-            physics(c - 1)
+        physics(c - 1)
     physics(chunks - 1)
 
     for copy in halos + chalos:
@@ -234,8 +254,10 @@
             direct(d, c).wait_send()
         for d in range(half):
             to_mate(d, c).wait_send()
-    for d in range(1, levs):
-        total_copy(d).wait_send()
+    for d in range(1, half):
+        total_direct(d).wait_send()
+    for d in range(half):
+        total_mate(d).wait_send()
     for copy in halos + chalos:
         copy.wait_send()
 
@@ -307,11 +329,11 @@
             vmem((R, levs * L, C), BF16),
             vmem((L * R, 2 * C), BF16), vmem((L * R, 2 * C), BF16),
             vmem((2, srows, C), F32),
-            vmem((R, C), F32), vmem((levs - 1, R, C), F32),
+            vmem((levs, R, C), F32),
             vmem((2, R, C), F32),
             dma((8,)),
             dma((max(half - 1, 1), chunks)), dma((max(half - 1, 1), chunks)), dma((half, chunks)), dma((half, chunks)),
-            dma((levs - 1,)), dma((levs - 1,)), dma((2,)), dma((2,)), dma((2,)), dma((2,)),
+            dma((max(half - 1, 1),)), dma((max(half - 1, 1),)), dma((half,)), dma((half,)), dma((2,)), dma((2,)), dma((2,)), dma((2,)),
         ],
         compiler_params=pltpu.CompilerParams(
             collective_id=0, has_side_effects=True, vmem_limit_bytes=24 * 1024 * 1024

time: 20 us -> 17.7 us (0.89); the launches traced: 19.9 us -> 17.4 us
  Pallas kernels: 19.3 us -> 16.7 us
    pallas_call x1, Pallas kernels: 17.8 us -> 15.3 us  [shards(): pl.pallas_call(functools.partial(kernel, (levs, tiles, L, R, C, S)), out_...]
where the time goes in v4:
time: 17.7 us; the launch traced here: 17.4 us
  Pallas kernels  16.7 us (94%)
  between operations  0.64 us (4%)
    pallas_call x1, Pallas kernels, shards(): pl.pallas_call(functools.partial(kernel, (levs, tiles, L, R, C, S)), out_...  15.3 us
    pallas_call x1, Pallas kernels, shards(): pl.pallas_call(finish_kernel, out_shape=(jax.ShapeDtypeStruct(flat, F32),...  1.45 us

profile of v4, /device:TPU:0, one launch (start us, length us, event | category | flops | bytes accessed | tf_op | source)
XLA Modules:
  0.0 17.4 jit_solution(2355555931874229586)
XLA Ops:
  0.6 15.3 %shard_map.103 = (f32[1024,128]{1,0:T(8,128)S(1)}, f32[1024,128]{1,0:T(8,128)S(1)}, f32[1024,128]{1,0:T(8,128)S(1)}, f32[2,128,128]{2,1,0:T(8,128)S(1)}, f32[2,3...) custom-call(f32[1024,128]{1,0:T(8,128)} %bitcast.5, f32[1024,128]{1,0:T(8,128)} %bitcast.6, f32[1024,128]{1,0:T(8,128)} %bitcast.7, ...), custom_call_target="tpu_custom_call" | custom-call | flops 1000000000 | bytes 4000000 | tf_op jit(solution)/shard_map/pallas_call | solution.py:317
  15.9 1.5 %shard_map.104 = (f32[1024,128]{1,0:T(8,128)}, f32[1024,128]{1,0:T(8,128)}, bf16[32,32,128]{2,1,0:T(8,128)(2,1)}) custom-call(f32[1024,128]{1,0:T(8,128)S(1)} %get-tuple-element.12.p_s, f32[1024,128]{1,0:T(8,128)S(1)} %get-tuple-element.13.v_s, f32[1024,128]{1,0:T(8,128)S(1)} %get-tuple-element.14.heat, f32[2,128,128]{2,1,0:T(8,128)S(1)} %get-tuple-element.15.pack, ...), custom_call_target="tpu_custom_call" | custom-call | flops 1000000 | bytes 3000000 | tf_op jit(solution)/shard_map/pallas_call | solution.py:351

commit v5 on v4

--- a/solution.py
+++ b/solution.py
@@ -57,10 +57,10 @@
 def kernel(
     dims,
     theta, thick, wind, surf, trig, clos, wts, operator,
-    p_s, v_s, heat, pack_in, cmain, cpack_in,
-    theta_v, thick_v, wind_v, surf_v, trig_v, clos_v, w_v, op_v, mhi_v, mlo_v,
-    gath, xh, xl, pack, tot, cpack,
-    in_sem, dir_send, dir_recv, par_send, par_recv,
+    p_s, v_s, heat,
+    theta_3d, thick_v, wind_v, surf_v, trig_v, clos_v, w_v, op_v, mhi_v, mlo_v,
+    gath, xh, xl, pack, pack_in, tot, cpack, cpack_in,
+    theta_sem, in_sem, dir_send, dir_recv, par_send, par_recv,
     tot_send, tot_recv, totm_send, totm_recv, halo_send, halo_recv, chalo_send, chalo_recv,
 ):
     levs, tiles, L, R, C, S = dims
@@ -72,18 +72,25 @@
     me = lax.axis_index("lev")
     here = lax.axis_index("tile")
     mate = me + 1 - 2 * (me % 2)
+    theta_v = theta_3d.reshape(L * R, C)
     right, left = (here + 1) % tiles, (here + tiles - 1) % tiles
 
     loads = [
         pltpu.make_async_copy(src, dst, in_sem.at[i])
         for i, (src, dst) in enumerate(
             [
-                (theta, theta_v), (thick, thick_v), (surf, surf_v), (wind, wind_v), (operator, op_v),
+                (thick, thick_v), (surf, surf_v), (wind, wind_v), (operator, op_v),
                 (wts.at[:, pl.ds(pl.multiple_of(me * L, 16), L), :], w_v), (trig, trig_v), (clos, clos_v),
             ]
         )
     ]
-    for copy in loads:
+    theta_loads = [
+        pltpu.make_async_copy(
+            theta.at[:, pl.ds(c * CHUNK, CHUNK), :], theta_3d.at[:, pl.ds(c * CHUNK, CHUNK), :], theta_sem.at[c]
+        )
+        for c in range(chunks)
+    ]
+    for copy in theta_loads + loads:
         copy.start()
     barrier = pltpu.get_barrier_semaphore()
     for d in range(1, levs):
@@ -128,16 +135,14 @@
         owner = ((mate if inward else me) + levs - 2 * d) % levs
         return total_copy(owner, totm_send.at[d], totm_recv.at[d], mate)
 
-    loads[0].wait()
-    loads[1].wait()
-
     def column(i, total):
         rows = pl.ds(pl.multiple_of((L - 1 - i) * R, R), R)
         return total + theta_v[rows, :] * thick_v[rows, :] * LEVELS ** (-0.5)
 
-    tot[me] = lax.fori_loop(0, L, column, jnp.zeros((R, C), F32), unroll=8)
-
     for c in range(chunks):
+        if c == 0:
+            theta_loads[0].wait()
+
         def relayout(i, _, c=c):
             r = c * CHUNK + i
             gath[r, slot_of(me), :] = theta_v[pl.ds(r, L, stride=R), :].astype(BF16)
@@ -146,14 +151,18 @@
         lax.fori_loop(0, CHUNK, relayout, 0, unroll=True)
         if c == 0:
             pl.semaphore_wait(barrier, levs + 1)
+        for d in range(1, half):
+            direct(d, c).start()
+        to_mate(0, c).start()
+        if c == 0:
+            for copy in theta_loads[1:] + loads[:1]:
+                copy.wait()
+            tot[me] = lax.fori_loop(0, L, column, jnp.zeros((R, C), F32), unroll=8)
             for d in range(1, half):
                 total_direct(d).start()
             total_mate(0).start()
-        for d in range(1, half):
-            direct(d, c).start()
-        to_mate(0, c).start()
-
-    for i in (2, 3):
+
+    for i in (1, 2):
         loads[i].wait()
 
     def level(i, total):
@@ -166,7 +175,7 @@
 
     lax.fori_loop(0, L, level, jnp.zeros((R, C), F32), unroll=4)
 
-    loads[4].wait()
+    loads[3].wait()
     mhi_v[...], mlo_v[...] = split(op_v[...])
     per = 2
     for step in range(slots // per):
@@ -211,15 +220,13 @@
         carry = carry + jnp.where(owner > me, tot[owner], 0.0)
     ch, cl = split(carry)
     yc = dot(ch, mhi_v[0:C, :]) + dot(cl, mhi_v[0:C, :]) + dot(ch, mlo_v[0:C, :])
-    cmain[0] = yc[:, 0:C]
-    cmain[1] = yc[:, C : 2 * C]
     cpack[0] = yc[:, 2 * C : 3 * C]
     cpack[1] = yc[:, 3 * C : 4 * C]
     chalos = [side_copy(cpack, cpack_in, chalo_send, chalo_recv, side) for side in range(2)]
     for copy in chalos:
         copy.start()
 
-    for i in (5, 6, 7):
+    for i in (4, 5, 6):
         loads[i].wait()
 
     def physics(c):
@@ -242,13 +249,31 @@
 
         lax.fori_loop(0, CHUNK // 2, pair, 0, unroll=True)
 
+    def finish():
+        for copy in halos + chalos:
+            copy.wait_recv()
+
+        def edges(to_left, to_right, start, rows):
+            at = lax.broadcasted_iota(jnp.int32, (rows, C), 1)
+            first = pltpu.roll(to_right, (C - start) % C, 1)
+            last = pltpu.roll(to_left, (2 * C - H - start) % C, 1)
+            return jnp.where(at < H, first, jnp.where(at >= C - H, last, 0.0))
+
+        common = [yc[:, f * C : (f + 1) * C] + edges(cpack_in[0], cpack_in[1], f * H, R) for f in range(2)]
+        for g in range(slots):
+            rows = pl.ds(g * srows, srows)
+            for f, held in enumerate((p_s, v_s)):
+                fix = edges(pack_in[0], pack_in[1], g * SLOT + f * H, srows)
+                many = (held[rows, :] + fix).reshape(srows // R, R, C) + common[f][None]
+                held[rows, :] = many.reshape(srows, C)
+
     for c in range(1, chunks):
+        if c == chunks - 1:
+            finish()
         forward(c)
         physics(c - 1)
     physics(chunks - 1)
 
-    for copy in halos + chalos:
-        copy.wait_recv()
     for c in range(chunks):
         for d in range(1, half):
             direct(d, c).wait_send()
@@ -262,14 +287,15 @@
         copy.wait_send()
 
 
-def finish_kernel(p_s, v_s, heat, pack, cmain, cpack, p_out, v_out, h_out, done, hout, out_sem, hout_sem):
+def store_kernel(p_s, v_s, heat, p_out, v_out, h_out, hout, out_sem, hout_sem):
     L, R, C = hout.shape
-    slots = C // SLOT
-    srows = L * R // slots
-    H = SUBSTEPS
-    copies = []
-
-    def emit(o):
+    copies = [
+        pltpu.make_async_copy(held, out, out_sem.at[field])
+        for field, (held, out) in enumerate(((p_s, p_out), (v_s, v_out)))
+    ]
+    for copy in copies:
+        copy.start()
+    for o in range(R // PACK):
         rows = pl.ds(o * PACK, PACK)
 
         def one(k, _):
@@ -280,25 +306,6 @@
         copy = pltpu.make_async_copy(hout.at[:, rows, :], h_out.at[:, rows, :], hout_sem.at[o])
         copy.start()
         copies.append(copy)
-
-    def edges(to_left, to_right, start, rows):
-        at = lax.broadcasted_iota(jnp.int32, (rows, C), 1)
-        first = pltpu.roll(to_right, (C - start) % C, 1)
-        last = pltpu.roll(to_left, (2 * C - H - start) % C, 1)
-        return jnp.where(at < H, first, jnp.where(at >= C - H, last, 0.0))
-
-    for o in range(R // PACK):
-        emit(o)
-    common = [cmain[field] + edges(cpack[0], cpack[1], field * H, R) for field in range(2)]
-    for g in range(slots):
-        rows = pl.ds(g * srows, srows)
-        for field, (held, out) in enumerate(((p_s, p_out), (v_s, v_out))):
-            fix = edges(pack[0], pack[1], g * SLOT + field * H, srows)
-            many = (held[rows, :] + fix).reshape(srows // R, R, C) + common[field][None]
-            done[field, rows, :] = many.reshape(srows, C)
-            copy = pltpu.make_async_copy(done.at[field, rows, :], out.at[rows, :], out_sem.at[field, g])
-            copy.start()
-            copies.append(copy)
     for copy in copies:
         copy.wait()
 
@@ -318,20 +325,19 @@
         functools.partial(kernel, (levs, tiles, L, R, C, S)),
         out_shape=(
             vmem(flat, F32), vmem(flat, F32), vmem(flat, F32),
-            vmem((2, srows, C), F32), vmem((2, R, C), F32), vmem((2, R, C), F32),
         ),
         in_specs=[hbm] * 8,
-        out_specs=(near,) * 6,
+        out_specs=(near,) * 3,
         scratch_shapes=[
-            vmem(flat, F32), vmem(flat, F32), vmem(flat, F32),
+            vmem((L, R, C), F32), vmem(flat, F32), vmem(flat, F32),
             vmem((R, C), F32), vmem((R, C), jnp.int32), vmem((R, C), jnp.int32),
             vmem((S, L, levs * L), BF16), vmem((2 * C, 4 * C), F32), vmem((2 * C, 4 * C), BF16), vmem((2 * C, 4 * C), BF16),
             vmem((R, levs * L, C), BF16),
             vmem((L * R, 2 * C), BF16), vmem((L * R, 2 * C), BF16),
-            vmem((2, srows, C), F32),
+            vmem((2, srows, C), F32), vmem((2, srows, C), F32),
             vmem((levs, R, C), F32),
-            vmem((2, R, C), F32),
-            dma((8,)),
+            vmem((2, R, C), F32), vmem((2, R, C), F32),
+            dma((chunks,)), dma((7,)),
             dma((max(half - 1, 1), chunks)), dma((max(half - 1, 1), chunks)), dma((half, chunks)), dma((half, chunks)),
             dma((max(half - 1, 1),)), dma((max(half - 1, 1),)), dma((half,)), dma((half,)), dma((2,)), dma((2,)), dma((2,)), dma((2,)),
         ],
@@ -343,20 +349,20 @@
         *(
             pltpu.with_memory_space_constraint(value, pltpu.HBM)
             for value in (
-                theta.reshape(flat), thickness.reshape(flat), wind.reshape(flat), surface, trigger, closure,
+                theta, thickness.reshape(flat), wind.reshape(flat), surface, trigger, closure,
                 closure_weights, jnp.asarray(substep_operator(C)),
             )
         )
     )
     p, v, h = pl.pallas_call(
-        finish_kernel,
+        store_kernel,
         out_shape=(
             jax.ShapeDtypeStruct(flat, F32), jax.ShapeDtypeStruct(flat, F32), jax.ShapeDtypeStruct((L, R, C), BF16)
         ),
-        in_specs=[near] * 6,
+        in_specs=[near] * 3,
         out_specs=(hbm,) * 3,
         scratch_shapes=[
-            vmem((2,) + flat, F32), vmem((L, R, C), BF16), dma((2, slots)), dma((R // PACK,)),
+            vmem((L, R, C), BF16), dma((2,)), dma((R // PACK,)),
         ],
         compiler_params=pltpu.CompilerParams(vmem_limit_bytes=16 * 1024 * 1024),
         cost_estimate=pl.CostEstimate(flops=10**6, bytes_accessed=3 * 10**6, transcendentals=0),

time: 17.7 us -> 19.3 us (1.090)
  Pallas kernels: 16.7 us -> 18.4 us
    pallas_call x1, Pallas kernels: 15.3 us -> 17.3 us  [shards(): pl.pallas_call(functools.partial(kernel, (levs, tiles, L, R, C, S)), out_...]
    pallas_call x1, Pallas kernels: 1.45 us -> 1.08 us  [shards(): pl.pallas_call(store_kernel, out_shape=(jax.ShapeDtypeStruct(flat, F32),...]
where the time goes in v5:
time: 19.3 us; the launch traced here: 19 us
  Pallas kernels  18.4 us (95%)
  between operations  0.64 us (3%)
    pallas_call x1, Pallas kernels, shards(): pl.pallas_call(functools.partial(kernel, (levs, tiles, L, R, C, S)), out_...  17.3 us
    pallas_call x1, Pallas kernels, shards(): pl.pallas_call(store_kernel, out_shape=(jax.ShapeDtypeStruct(flat, F32),...  1.08 us

profile of v5, /device:TPU:0, one launch (start us, length us, event | category | flops | bytes accessed | tf_op | source)
XLA Modules:
  0.0 19.0 jit_solution(10520251447212071058)
XLA Ops:
  0.6 17.3 %shard_map.103 = (f32[1024,128]{1,0:T(8,128)S(1)}, f32[1024,128]{1,0:T(8,128)S(1)}, f32[1024,128]{1,0:T(8,128)S(1)}) custom-call(f32[32,32,128]{2,1,0:T(8,128)} %theta.1, f32[1024,128]{1,0:T(8,128)} %bitcast.4, f32[1024,128]{1,0:T(8,128)} %bitcast.5, f32[32,128]{1,0:T(8,128)} %surf.1, s32[32,128]{1,0:T(8,128)} %trig.1, s32[32,128]{1,0:T(8,128)} %clos.1, ...), custom_call_target="tpu_custom_call" | custom-call | flops 1000000000 | bytes 4000000 | tf_op jit(solution)/shard_map/pallas_call | solution.py:324
  17.9 1.1 %shard_map.104 = (f32[1024,128]{1,0:T(8,128)}, f32[1024,128]{1,0:T(8,128)}, bf16[32,32,128]{2,1,0:T(8,128)(2,1)}) custom-call(f32[1024,128]{1,0:T(8,128)S(1)} %get-tuple-element.9.p_s, f32[1024,128]{1,0:T(8,128)S(1)} %get-tuple-element.10.v_s, f32[1024,128]{1,0:T(8,128)S(1)} %get-tuple-element.11.heat), custom_call_target="tpu_custom_call" | custom-call | flops 1000000 | bytes 3000000 | tf_op jit(solution)/shard_map/pallas_call | solution.py:357
